TPU v7x, 256 devices: a whole 4x4x8 slice. The times are simulated.
256 devices in a mesh: span: 8 (over y, core), seq: 16 (over z_hi, x), mp: 2 (over z_lo).
Axes of the slice: x: 4, y: 4, z: 8 (z_hi: 4, z_lo: 2; z = z_hi * 2 + z_lo), core: 2. Of those that a mesh axis runs over, the one named last changes fastest.
Arguments:
- query: bfloat16 [8, 1024, 4096], P('span', 'seq', 'mp'), may hold values from -33 to 33, as said below
- key: bfloat16 [8, 1024, 4096], P('span', 'seq', 'mp'), may hold values from -33 to 33, as said below
- value: bfloat16 [8, 1024, 4096], P('span', 'seq', 'mp'), may hold values from -6 to 6
- cache_key: bfloat16 [8, 1024, 4096], P('span', 'seq', 'mp'), may hold values from -21 to 21
- cache_value: bfloat16 [8, 1024, 4096], P('span', 'seq', 'mp'), may hold values from -6 to 6
- q_gain: float32 [4096], P('mp'), may hold values from 0.1 to 1.9
- k_gain: float32 [4096], P('mp'), may hold values from 0.1 to 1.9
- gate_table: float32 [32, 4096], P(None, 'mp'), may hold values from 0.5 to 2
- span_order: int32 [8], replicated, may hold values from 0 to 31, as said below
- noise_step: int32 [8], replicated, may hold values from 0 to 31
- context_mask: int32 [32, 32], replicated, may hold values 0 or 1
Outputs:
- attended: bfloat16 [8, 1024, 4096], P('span', 'seq', 'mp')
Inputs may be any that keep to these rules, and one draw needn't show every extreme that they name: `query`: rows and columns carry different scales. `key`: rows and columns carry different scales. `span_order`: distinct positions.
All inputs are finite; a program needn't handle non-finite values.
Results may differ from a plain program's by a relative error of at most 0.018.
Values may be sent and summed in bfloat16 or wider, within the bound.
A program may use at most 128 MiB of HBM per device.

v0:
```python
import functools
import math

import jax
import jax.numpy as jnp
from jax import lax
from jax.experimental import pallas as pl
from jax.experimental.pallas import tpu as pltpu
from jax.sharding import PartitionSpec as P

MESH = pl.DeviceIdType.MESH
HEADS = 32
HD = 128
EPS = 1e-6
OUT_OF_MAX = 1e30
OUT_OF_SUM = 3e30


def exchange_and_attend(
    chips_y,
    ring_z,
    ring_x,
    query,
    key,
    value,
    cache_key,
    cache_value,
    q_gain,
    k_gain,
    gate_table,
    span_order,
    noise_step,
    context_mask,
    out,
    raw,
    normed,
    squares,
    gates,
    heads,
    cached,
    total,
    top,
    mass,
    done,
    load_sem,
    local_sem,
    mp_send,
    mp_recv,
    cache_send,
    cache_recv,
    head_send,
    head_recv,
    y_send,
    y_recv,
    core_send,
    core_recv,
    out_send,
    out_recv,
):
    span = lax.axis_index("span")
    seq = lax.axis_index("seq")
    mp = lax.axis_index("mp")
    y, core = span // 2, span % 2
    z, x = seq // ring_x, seq % ring_x
    members = ring_z * ring_x
    tokens = raw.shape[1]
    group = ring_x * tokens
    length = members * tokens
    width = HEADS * HD
    partner = (y * 2 + (1 - core), seq, mp)
    my_rows = pl.ds(pl.multiple_of(seq * tokens, tokens), tokens)
    my_columns = pl.ds(pl.multiple_of(seq * HD, HD), HD)

    def peer(dz, dx):
        return lax.rem(z + dz, ring_z) * ring_x + lax.rem(x + dx, ring_x)

    def group_rows(dz):
        return pl.ds(pl.multiple_of(lax.rem(z + ring_z - dz, ring_z) * group, group), group)

    barrier = pltpu.get_barrier_semaphore()

    def greet(step, carry):
        other = lax.rem(seq + step, members)
        pl.semaphore_signal(barrier, inc=1, device_id=(span, other, mp), device_id_type=MESH)
        return carry

    lax.fori_loop(1, members, greet, 0)
    for dy in range(1, chips_y):
        pl.semaphore_signal(
            barrier,
            inc=1,
            device_id=(lax.rem(y + dy, chips_y) * 2 + core, seq, mp),
            device_id_type=MESH,
        )
    pl.semaphore_signal(barrier, inc=1, device_id=partner, device_id_type=MESH)
    pl.semaphore_signal(barrier, inc=1, device_id=(span, seq, 1 - mp), device_id_type=MESH)

    loads = [
        pltpu.make_async_copy(query.at[0], raw.at[0], load_sem.at[0]),
        pltpu.make_async_copy(key.at[0], raw.at[1], load_sem.at[1]),
        pltpu.make_async_copy(gate_table.at[:, my_columns], gates, load_sem.at[2]),
    ]
    for load in loads:
        load.start()
    owns = [
        pltpu.make_async_copy(
            cache_key.at[0, :, my_columns], cached.at[0, 0, my_rows], local_sem.at[0]
        ),
        pltpu.make_async_copy(
            cache_value.at[0, :, my_columns], cached.at[0, 1, my_rows], local_sem.at[1]
        ),
        pltpu.make_async_copy(value.at[0, :, my_columns], heads.at[2, my_rows], local_sem.at[2]),
    ]
    for own in owns:
        own.start()
    pl.semaphore_wait(barrier, members - 1 + chips_y - 1 + 2)

    for dz in range(ring_z):

        def send_cache(dx, carry, dz=dz):
            other = peer(dz, dx)
            columns = pl.ds(pl.multiple_of(other * HD, HD), HD)
            for which, source in enumerate((cache_key, cache_value)):
                pltpu.make_async_remote_copy(
                    src_ref=source.at[0, :, columns],
                    dst_ref=cached.at[0, which, my_rows],
                    send_sem=cache_send.at[which],
                    recv_sem=cache_recv.at[dz],
                    device_id=(span, other, mp),
                    device_id_type=MESH,
                ).start()
            return carry

        lax.fori_loop(1 if dz == 0 else 0, ring_x, send_cache, 0)

    loads[0].wait()
    loads[1].wait()
    lane = lax.broadcasted_iota(jnp.int32, (tokens, HD), 1)

    def row_squares(which):
        wide = raw[which].astype(jnp.float32)
        return jnp.sum(wide * wide, axis=-1, keepdims=True)

    squares[0] = jnp.where(lane < HD // 2, row_squares(0), row_squares(1))
    swap = pltpu.make_async_remote_copy(
        src_ref=squares.at[0],
        dst_ref=squares.at[1],
        send_sem=mp_send,
        recv_sem=mp_recv,
        device_id=(span, seq, 1 - mp),
        device_id_type=MESH,
    )
    swap.start()
    swap.wait()
    factors = lax.rsqrt((squares[0] + squares[1]) / width + EPS)
    scale = math.log2(math.e) / math.sqrt(HD)

    def send_heads(which, source):
        def step(hop, carry):
            other = lax.rem(seq + hop, members)
            columns = pl.ds(pl.multiple_of(other * HD, HD), HD)
            pltpu.make_async_remote_copy(
                src_ref=source.at[:, columns],
                dst_ref=heads.at[which, my_rows],
                send_sem=head_send.at[which],
                recv_sem=head_recv.at[which],
                device_id=(span, other, mp),
                device_id_type=MESH,
            ).start()
            return carry

        lax.fori_loop(1, members, step, 0)

    for which, gain in enumerate((q_gain, k_gain)):
        at = which * (HD // 2)
        factor = factors[:, at : at + 1] * (scale if which == 0 else 1.0)
        normed[which] = (
            raw[which].astype(jnp.float32) * factor * gain[...][None, :]
        ).astype(jnp.bfloat16)
        own = pltpu.make_async_copy(
            normed.at[which, :, my_columns], heads.at[which, my_rows], local_sem.at[3 + which]
        )
        own.start()
        owns.append(own)
        send_heads(which, normed.at[which])
    send_heads(2, value.at[0])

    owns[0].wait()
    owns[1].wait()
    for dz in range(ring_z):
        count = (ring_x - 1 if dz == 0 else ring_x) * tokens
        arrived = cached.at[0, :, pl.ds(0, count)]
        pltpu.make_async_copy(arrived, arrived, cache_recv.at[dz]).wait()
        part = cached.at[0, :, group_rows(dz)]
        for dy in (1, 3, 2):
            pltpu.make_async_remote_copy(
                src_ref=part,
                dst_ref=cached.at[2 * (chips_y - dy), :, group_rows(dz)],
                send_sem=y_send.at[dy - 1],
                recv_sem=y_recv.at[chips_y - dy - 1, dz],
                device_id=(lax.rem(y + dy, chips_y) * 2 + core, seq, mp),
                device_id_type=MESH,
            ).start()
        pltpu.make_async_remote_copy(
            src_ref=part,
            dst_ref=cached.at[1, :, group_rows(dz)],
            send_sem=core_send.at[0],
            recv_sem=core_recv.at[0],
            device_id=partner,
            device_id_type=MESH,
        ).start()

    def attend(rows, keys, values, hide_max, hide_sum):
        scores = lax.dot_general(
            heads[0, rows],
            keys,
            (((1,), (1,)), ((), ())),
            preferred_element_type=jnp.float32,
        )
        before = top[rows]
        now = jnp.maximum(before, jnp.max(scores, axis=-1, keepdims=True) - hide_max)
        shift = (now + hide_sum)[:, :1]
        weights = jnp.exp2(scores - shift)
        shrink = jnp.exp2(before - now)
        top[rows] = now
        mass[rows] = mass[rows] * shrink + jnp.sum(weights, axis=-1, keepdims=True)
        total[rows] = total[rows] * shrink + jnp.dot(
            weights.astype(jnp.bfloat16), values, preferred_element_type=jnp.float32
        )

    def block(slot, dy, dc):
        other = lax.rem(y + dy, chips_y) * 2 + lax.rem(core + dc, 2)
        mine, theirs = span_order[span], span_order[other]
        seen = jnp.where(theirs < mine, context_mask[mine, theirs], 0)
        hide_max = jnp.where(seen > 0, 0.0, OUT_OF_MAX).astype(jnp.float32)
        hide_sum = jnp.where(seen > 0, 0.0, OUT_OF_SUM).astype(jnp.float32)

        def part(index, carry):
            rows = pl.ds(pl.multiple_of(index * group, group), group)
            attend(rows, cached[slot, 0], cached[slot, 1], hide_max, hide_sum)
            return carry

        lax.fori_loop(0, ring_z, part, 0)

    top[...] = jnp.full_like(top, -3e38)
    mass[...] = jnp.zeros_like(mass)
    total[...] = jnp.zeros_like(total)
    arrived = heads.at[0, pl.ds(0, length - tokens)]
    owns[3].wait()
    pltpu.make_async_copy(arrived, arrived, head_recv.at[0]).wait()
    whole = cached.at[1]
    pltpu.make_async_copy(whole, whole, core_recv.at[0]).wait()
    block(1, 0, 1)
    for dy in (1, 3, 2):
        for dz in range(ring_z):
            part = cached.at[2 * dy, :, group_rows(dz)]
            pltpu.make_async_copy(part, part, y_recv.at[dy - 1, dz]).wait()
            pltpu.make_async_remote_copy(
                src_ref=part,
                dst_ref=cached.at[2 * dy + 1, :, group_rows(dz)],
                send_sem=core_send.at[dy],
                recv_sem=core_recv.at[dy],
                device_id=partner,
                device_id_type=MESH,
            ).start()
        block(2 * dy, dy, 0)
        whole = cached.at[2 * dy + 1]
        pltpu.make_async_copy(whole, whole, core_recv.at[dy]).wait()
        block(2 * dy + 1, dy, 1)

    loads[2].wait()
    for which in (1, 2):
        owns[2 if which == 2 else 4].wait()
        arrived = heads.at[which, pl.ds(0, length - tokens)]
        pltpu.make_async_copy(arrived, arrived, head_recv.at[which]).wait()
    steps = lax.broadcasted_iota(jnp.int32, gates.shape, 0)
    gate = jnp.sum(jnp.where(steps == noise_step[span], gates[...], 0.0), axis=0, keepdims=True)
    for dz in (2, 1, 3, 0):
        to_z = lax.rem(z + dz, ring_z)
        rows = pl.ds(pl.multiple_of(to_z * group, group), group)
        attend(rows, heads[1], heads[2], 0.0, 0.0)
        attended = total[rows] / mass[rows]
        factor = lax.rsqrt(jnp.mean(attended * attended, axis=-1, keepdims=True) + EPS)
        done[rows] = (attended * factor * gate).astype(jnp.bfloat16)

        def send_out(dx, carry, dz=dz):
            other = peer(dz, dx)
            pltpu.make_async_remote_copy(
                src_ref=done.at[pl.ds(pl.multiple_of(other * tokens, tokens), tokens)],
                dst_ref=out.at[0, :, my_columns],
                send_sem=out_send,
                recv_sem=out_recv,
                device_id=(span, other, mp),
                device_id_type=MESH,
            ).start()
            return carry

        lax.fori_loop(1 if dz == 0 else 0, ring_x, send_out, 0)
    keep = pltpu.make_async_copy(done.at[my_rows], out.at[0, :, my_columns], local_sem.at[5])
    keep.start()
    keep.wait()

    sent = heads.at[0, pl.ds(0, length - tokens)]
    for sem in (cache_send.at[0], cache_send.at[1], head_send.at[0], head_send.at[1], head_send.at[2]):
        pltpu.make_async_copy(sent, sent, sem).wait()
    whole = cached.at[0]
    for dy in range(1, chips_y):
        pltpu.make_async_copy(whole, whole, y_send.at[dy - 1]).wait()
    for dy in range(chips_y):
        pltpu.make_async_copy(whole, whole, core_send.at[dy]).wait()
    pltpu.make_async_copy(sent, sent, out_send).wait()
    pltpu.make_async_copy(sent, sent, out_recv).wait()


def shards(
    query,
    key,
    value,
    cache_key,
    cache_value,
    q_gain,
    k_gain,
    gate_table,
    span_order,
    noise_step,
    context_mask,
):
    spans, members = lax.axis_size("span"), lax.axis_size("seq")
    chips_y = spans // 2
    ring_x = 4
    ring_z = members // ring_x
    tokens, columns = query.shape[1:]
    length = tokens * members
    dma = pltpu.SemaphoreType.DMA
    anywhere = pl.BlockSpec(memory_space=pl.ANY)
    in_vmem = pl.BlockSpec(memory_space=pltpu.VMEM)
    in_smem = pl.BlockSpec(memory_space=pltpu.SMEM)
    bf16, f32 = jnp.bfloat16, jnp.float32
    return pl.pallas_call(
        functools.partial(exchange_and_attend, chips_y, ring_z, ring_x),
        out_shape=jax.ShapeDtypeStruct(query.shape, bf16),
        in_specs=[anywhere] * 5 + [in_vmem] * 2 + [anywhere] + [in_smem] * 3,
        out_specs=in_vmem,
        scratch_shapes=[
            pltpu.VMEM((2, tokens, columns), bf16),
            pltpu.VMEM((2, tokens, columns), bf16),
            pltpu.VMEM((2, tokens, HD), f32),
            pltpu.VMEM((gate_table.shape[0], HD), f32),
            pltpu.VMEM((3, length, HD), bf16),
            pltpu.VMEM((spans, 2, length, HD), bf16),
            pltpu.VMEM((length, HD), f32),
            pltpu.VMEM((length, HD), f32),
            pltpu.VMEM((length, HD), f32),
            pltpu.VMEM((length, HD), bf16),
            dma((3,)),
            dma((6,)),
            dma,
            dma,
            dma((2,)),
            dma((ring_z,)),
            dma((3,)),
            dma((3,)),
            dma((chips_y - 1,)),
            dma((chips_y - 1, ring_z)),
            dma((chips_y,)),
            dma((chips_y,)),
            dma,
            dma,
        ],
        compiler_params=pltpu.CompilerParams(
            collective_id=0, has_side_effects=True, vmem_limit_bytes=48 << 20
        ),
        name="exchange_and_attend",
    )(
        query,
        key,
        value,
        cache_key,
        cache_value,
        q_gain,
        k_gain,
        gate_table,
        span_order,
        noise_step,
        context_mask,
    )


def solution(mesh):
    placed = (
        P("span", "seq", "mp"),
        P("span", "seq", "mp"),
        P("span", "seq", "mp"),
        P("span", "seq", "mp"),
        P("span", "seq", "mp"),
        P("mp"),
        P("mp"),
        P(None, "mp"),
        P(),
        P(),
        P(),
    )
    return jax.shard_map(
        shards, mesh=mesh, in_specs=placed, out_specs=P("span", "seq", "mp"), check_vma=False
    )
```

profile of v0, /device:TPU:2, one launch (start us, length us, event | category | flops | bytes accessed | tf_op | source)
XLA Modules:
  0.0 84.7 jit_solution(5338505048208841753)
XLA Ops:
  0.0 0.0 copy-start
  0.0 0.9 %copy-done = bf16[1,64,2048]{2,1,0:T(8,128)(2,1)S(1)} copy-done((bf16[1,64,2048]{2,1,0:T(8,128)(2,1)S(1)}, bf16[1,64,2048]{2,1,0:T(8,128)(2,1)}, u32[]{:S(2)}) %copy-start) | copy-done | bytes 262168
  1.0 0.0 copy-start.1
  1.0 0.9 %copy-done.1 = bf16[1,64,2048]{2,1,0:T(8,128)(2,1)S(1)} copy-done((bf16[1,64,2048]{2,1,0:T(8,128)(2,1)S(1)}, bf16[1,64,2048]{2,1,0:T(8,128)(2,1)}, u32[]{:S(2)}) %copy-start.1) | copy-done | bytes 262168
  1.9 0.0 copy-start.2
  1.9 0.9 %copy-done.2 = bf16[1,64,2048]{2,1,0:T(8,128)(2,1)S(1)} copy-done((bf16[1,64,2048]{2,1,0:T(8,128)(2,1)S(1)}, bf16[1,64,2048]{2,1,0:T(8,128)(2,1)}, u32[]{:S(2)}) %copy-start.2) | copy-done | bytes 262168
  2.9 0.0 copy-start.3
  2.9 0.9 %copy-done.3 = bf16[1,64,2048]{2,1,0:T(8,128)(2,1)S(1)} copy-done((bf16[1,64,2048]{2,1,0:T(8,128)(2,1)S(1)}, bf16[1,64,2048]{2,1,0:T(8,128)(2,1)}, u32[]{:S(2)}) %copy-start.3) | copy-done | bytes 262168
  3.8 0.0 copy-start.4
  3.8 0.9 %copy-done.4 = bf16[1,64,2048]{2,1,0:T(8,128)(2,1)S(1)} copy-done((bf16[1,64,2048]{2,1,0:T(8,128)(2,1)S(1)}, bf16[1,64,2048]{2,1,0:T(8,128)(2,1)}, u32[]{:S(2)}) %copy-start.4) | copy-done | bytes 262168
  4.8 0.0 copy-start.5
  4.8 0.9 %copy-done.5 = f32[32,2048]{1,0:T(8,128)S(1)} copy-done((f32[32,2048]{1,0:T(8,128)S(1)}, f32[32,2048]{1,0:T(8,128)}, u32[]{:S(2)}) %copy-start.5) | copy-done | bytes 262168
  5.7 0.0 copy-start.6
  5.7 0.7 copy-done.6
  6.4 0.0 copy-start.7
  6.4 0.7 copy-done.7
  7.1 0.0 copy-start.8
  7.1 0.7 copy-done.8
  7.8 0.0 copy-start.9
  7.8 0.7 copy-done.9
  8.5 0.0 copy-start.10
  8.5 0.7 copy-done.10
  9.1 74.8 %exchange_and_attend.1 = bf16[1,64,2048]{2,1,0:T(8,128)(2,1)S(1)} custom-call(bf16[1,64,2048]{2,1,0:T(8,128)(2,1)S(1)} %copy-done, bf16[1,64,2048]{2,1,0:T(8,128)(2,1)S(1)} %copy-done.1, bf16[1,64,2048]{2,1,0:T(8,128)(2,1)S(1)} %copy-done.2, bf16[1,64,2048]{2,1,0:T(8,128)(2,1)S(1)} %copy-done.3, bf16[1,64,2048]{2,1,0:T(8,128)(2,1)S(1)} %copy-done.4, ...), custom_call_target="tpu_custom_call" | custom-call | tf_op jit(solution)/shard_map/exchange_and_attend/pallas_call | solution.py:339
  84.0 0.7 copy.13
Async XLA Ops:
  0.0 0.9 %copy-start = (bf16[1,64,2048]{2,1,0:T(8,128)(2,1)S(1)}, bf16[1,64,2048]{2,1,0:T(8,128)(2,1)}, u32[]{:S(2)}) copy-start(bf16[1,64,2048]{2,1,0:T(8,128)(2,1)} %query.1) | copy-start | bytes 786436
  1.0 0.9 %copy-start.1 = (bf16[1,64,2048]{2,1,0:T(8,128)(2,1)S(1)}, bf16[1,64,2048]{2,1,0:T(8,128)(2,1)}, u32[]{:S(2)}) copy-start(bf16[1,64,2048]{2,1,0:T(8,128)(2,1)} %key.1) | copy-start | bytes 786436
  1.9 0.9 %copy-start.2 = (bf16[1,64,2048]{2,1,0:T(8,128)(2,1)S(1)}, bf16[1,64,2048]{2,1,0:T(8,128)(2,1)}, u32[]{:S(2)}) copy-start(bf16[1,64,2048]{2,1,0:T(8,128)(2,1)} %value.1) | copy-start | bytes 786436
  2.9 0.9 %copy-start.3 = (bf16[1,64,2048]{2,1,0:T(8,128)(2,1)S(1)}, bf16[1,64,2048]{2,1,0:T(8,128)(2,1)}, u32[]{:S(2)}) copy-start(bf16[1,64,2048]{2,1,0:T(8,128)(2,1)} %cache_key.1) | copy-start | bytes 786436
  3.8 0.9 %copy-start.4 = (bf16[1,64,2048]{2,1,0:T(8,128)(2,1)S(1)}, bf16[1,64,2048]{2,1,0:T(8,128)(2,1)}, u32[]{:S(2)}) copy-start(bf16[1,64,2048]{2,1,0:T(8,128)(2,1)} %cache_value.1) | copy-start | bytes 786436
  4.8 0.9 %copy-start.5 = (f32[32,2048]{1,0:T(8,128)S(1)}, f32[32,2048]{1,0:T(8,128)}, u32[]{:S(2)}) copy-start(f32[32,2048]{1,0:T(8,128)} %gate_table.1) | copy-start | bytes 786436
  5.7 0.7 copy-start.6
  6.4 0.7 copy-start.7
  7.1 0.7 copy-start.8
  7.8 0.7 copy-start.9
  8.5 0.7 copy-start.10
where the time goes:
time: 85.4 us; the launch traced here: 84.7 us
  Pallas kernels  74.8 us (88%)
  local copies, waits for them, and re-layouts  9.82 us (11%)
    pallas_call x1, Pallas kernels, shards(): pl.pallas_call(functools.partial(exchange_and_attend, chips_y, ring_z, ri...  74.8 us
    unnamed x23, local copies, waits for them, and re-layouts  9.82 us

commit v1 on v0

v1 whole, which is shorter than its diff:
```python
import functools
import math

import jax
import jax.numpy as jnp
from jax import lax
from jax.experimental import pallas as pl
from jax.experimental.pallas import tpu as pltpu
from jax.sharding import PartitionSpec as P

MESH = pl.DeviceIdType.MESH
HEADS = 32
HD = 128
EPS = 1e-6
Z_ORDER = (0, 1, 3, 2)
HALVES = 2
EARLY = 3
BLOCKS = ((0, 1), (1, 0), (3, 0), (1, 1), (3, 1), (2, 0), (2, 1))
OWN = len(BLOCKS)
STAGED = OWN + 1
NEAR = (2, 1)
FAR = 5
ONES = 16
WAITS = (
    (1, (("core", 1, 0),)),
    (2, (("core", 2, 0), ("staged", 3))),
    (3, (("near", 2), ("far", 1))),
    (4, (("core", 3, 0), ("far", 2))),
    (5, (("near", 3),)),
    (6, (("core", 0, 1),)),
    (8, (("far", 3),)),
    (9, (("core", 1, 1),)),
    (10, (("core", 2, 1),)),
    (12, (("core", 3, 1),)),
)
OUT_OF_MAX = 1e30
OUT_OF_SUM = 3e30


def exchange_and_attend(
    chips_y,
    ring_z,
    ring_x,
    query,
    key,
    value,
    cache_key,
    cache_value,
    q_gain,
    k_gain,
    gate_table,
    span_order,
    noise_step,
    context_mask,
    result,
    gains,
    order,
    noise,
    mask,
    raw,
    normed,
    squares,
    gates,
    hide,
    queries,
    queries_t,
    blocks,
    scores,
    own_scores,
    total,
    top,
    mass,
    done,
    load_sem,
    local_sem,
    mp_send,
    mp_recv,
    cache_send,
    cache_recv,
    head_send,
    head_recv,
    near_send,
    near_recv,
    far_send,
    far_recv,
    core_send,
    core_recv,
    out_send,
    out_recv,
):
    out = result
    span = lax.axis_index("span")
    seq = lax.axis_index("seq")
    mp = lax.axis_index("mp")
    y, core = span // 2, span % 2
    z, x = seq // ring_x, seq % ring_x
    members = ring_z * ring_x
    tokens = raw.shape[1]
    group = ring_x * tokens
    length = members * tokens
    width = HEADS * HD
    partner = (y * 2 + (1 - core), seq, mp)
    my_rows = pl.ds(pl.multiple_of(seq * tokens, tokens), tokens)
    my_columns = pl.ds(pl.multiple_of(seq * HD, HD), HD)

    def peer(dz, dx):
        return lax.rem(z + dz, ring_z) * ring_x + lax.rem(x + dx, ring_x)

    def stage_rows(stage):
        return pl.ds(stage * group, group)

    def landing(stage):
        return pl.ds(pl.multiple_of(stage * group + x * tokens, tokens), tokens)

    barrier = pltpu.get_barrier_semaphore()

    def greet(step, carry):
        other = lax.rem(seq + step, members)
        pl.semaphore_signal(barrier, inc=1, device_id=(span, other, mp), device_id_type=MESH)
        return carry

    lax.fori_loop(1, members, greet, 0)
    for dy in range(1, chips_y):
        pl.semaphore_signal(
            barrier,
            inc=1,
            device_id=(lax.rem(y + dy, chips_y) * 2 + core, seq, mp),
            device_id_type=MESH,
        )
    pl.semaphore_signal(barrier, inc=1, device_id=partner, device_id_type=MESH)
    pl.semaphore_signal(barrier, inc=1, device_id=(span, seq, 1 - mp), device_id_type=MESH)

    loads = [
        pltpu.make_async_copy(source, target, load_sem.at[index])
        for index, (source, target) in enumerate(
            (
                (query.at[0], raw.at[0]),
                (key.at[0], raw.at[1]),
                (q_gain, gains.at[0]),
                (k_gain, gains.at[1]),
                (gate_table.at[:, my_columns], gates),
                (span_order, order),
                (noise_step, noise),
                (context_mask, mask),
                (cache_key.at[0], raw.at[2]),
                (cache_value.at[0], raw.at[3]),
                (value.at[0], raw.at[4]),
            )
        )
    ]
    for load in loads:
        load.start()
    loads[0].wait()
    loads[1].wait()
    lane = lax.broadcasted_iota(jnp.int32, (tokens, HD), 1)

    def row_squares(which):
        wide = raw[which].astype(jnp.float32)
        return jnp.sum(wide * wide, axis=-1, keepdims=True)

    squares[0] = jnp.where(lane < HD // 2, row_squares(0), row_squares(1))
    for load in loads[8:]:
        load.wait()
    owns = [
        pltpu.make_async_copy(
            raw.at[2, :, my_columns], blocks.at[STAGED, 0, landing(0)], local_sem.at[0]
        ),
        pltpu.make_async_copy(
            raw.at[3, :, my_columns], blocks.at[STAGED, 1, landing(0)], local_sem.at[1]
        ),
        pltpu.make_async_copy(raw.at[4, :, my_columns], blocks.at[OWN, 1, landing(0)], local_sem.at[2]),
    ]
    for own in owns:
        own.start()
    pl.semaphore_wait(barrier, members - 1 + chips_y - 1 + 2)
    swap = pltpu.make_async_remote_copy(
        src_ref=squares.at[0],
        dst_ref=squares.at[1],
        send_sem=mp_send,
        recv_sem=mp_recv,
        device_id=(span, seq, 1 - mp),
        device_id_type=MESH,
    )
    swap.start()

    def send_caches(stage):
        dz = Z_ORDER[stage]

        def send(dx, carry):
            other = peer(dz, dx)
            columns = pl.ds(pl.multiple_of(other * HD, HD), HD)
            for which in range(2):
                pltpu.make_async_remote_copy(
                    src_ref=raw.at[2 + which, :, columns],
                    dst_ref=blocks.at[STAGED, which, landing(stage)],
                    send_sem=cache_send.at[which],
                    recv_sem=cache_recv.at[stage],
                    device_id=(span, other, mp),
                    device_id_type=MESH,
                ).start()
            return carry

        lax.fori_loop(1 if dz == 0 else 0, ring_x, send, 0)

    for stage in range(EARLY):
        send_caches(stage)

    def to_core(source, target, stage, index):
        pltpu.make_async_remote_copy(
            src_ref=blocks.at[source, :, stage_rows(stage)],
            dst_ref=blocks.at[target, :, stage_rows(stage)],
            send_sem=core_send.at[index],
            recv_sem=core_recv.at[index, stage * HALVES // ring_z],
            device_id=partner,
            device_id_type=MESH,
        ).start()

    def along_y(way):
        return (lax.rem(y + (1, chips_y - 1)[way], chips_y) * 2 + core, seq, mp)

    def pass_near(stage):
        for way, place in enumerate(NEAR):
            part = blocks.at[place, :, stage_rows(stage)]
            pltpu.make_async_copy(part, part, near_recv.at[way, stage]).wait()
            pltpu.make_async_remote_copy(
                src_ref=blocks.at[place, way, stage_rows(stage)],
                dst_ref=blocks.at[FAR, way, stage_rows(stage)],
                send_sem=far_send.at[way],
                recv_sem=far_recv.at[way, stage],
                device_id=along_y(way),
                device_id_type=MESH,
            ).start()
            to_core(place, place + 2, stage, place)

    def pass_far(stage):
        for way in range(2):
            part = blocks.at[FAR, way, stage_rows(stage)]
            pltpu.make_async_copy(part, part, far_recv.at[way, stage]).wait()
        to_core(FAR, FAR + 1, stage, 3)

    def await_core(index, half):
        rows = pl.ds(half * (length // HALVES), length // HALVES)
        part = blocks.at[(0, 3, 4, 6)[index], :, rows]
        pltpu.make_async_copy(part, part, core_recv.at[index, half]).wait()

    owns[0].wait()
    owns[1].wait()
    def pass_staged(stage):
        count = (ring_x - 1 if Z_ORDER[stage] == 0 else ring_x) * tokens
        arrived = blocks.at[STAGED, :, pl.ds(0, count)]
        pltpu.make_async_copy(arrived, arrived, cache_recv.at[stage]).wait()
        for way, place in enumerate(NEAR):
            pltpu.make_async_remote_copy(
                src_ref=blocks.at[STAGED, :, stage_rows(stage)],
                dst_ref=blocks.at[place, :, stage_rows(stage)],
                send_sem=near_send.at[way],
                recv_sem=near_recv.at[way, stage],
                device_id=along_y(way),
                device_id_type=MESH,
            ).start()
        to_core(STAGED, 0, stage, 0)

    pass_staged(0)

    swap.wait()
    loads[2].wait()
    loads[3].wait()
    factors = lax.rsqrt((squares[0] + squares[1]) / width + EPS)
    scale = math.log2(math.e) / math.sqrt(HD)

    def send_heads(which, source):
        for stage, dz in enumerate(Z_ORDER):

            def send(dx, carry, stage=stage, dz=dz):
                other = peer(dz, dx)
                columns = pl.ds(pl.multiple_of(other * HD, HD), HD)
                if which == 0:
                    target = queries.at[my_rows]
                else:
                    target = blocks.at[OWN, which - 1, landing(stage)]
                pltpu.make_async_remote_copy(
                    src_ref=source.at[:, columns],
                    dst_ref=target,
                    send_sem=head_send.at[which],
                    recv_sem=head_recv.at[which],
                    device_id=(span, other, mp),
                    device_id_type=MESH,
                ).start()
                return carry

            lax.fori_loop(1 if dz == 0 else 0, ring_x, send, 0)

    for which in range(2):
        at = which * (HD // 2)
        factor = factors[:, at : at + 1] * (scale if which == 0 else 1.0)
        normed[which] = (
            raw[which].astype(jnp.float32) * factor * gains[which][None, :]
        ).astype(jnp.bfloat16)
        own = pltpu.make_async_copy(
            normed.at[which, :, my_columns],
            queries.at[my_rows] if which == 0 else blocks.at[OWN, 0, landing(0)],
            local_sem.at[3 + which],
        )
        own.start()
        owns.append(own)
        send_heads(which, normed.at[which])
        if which == 0:
            for stage in range(EARLY, ring_z):
                send_caches(stage)
    send_heads(2, raw.at[4])

    pass_staged(1)
    pass_near(0)
    pass_staged(2)
    pass_near(1)
    pass_far(0)

    for load in loads[4:8]:
        load.wait()
    for place, (dy, dc) in enumerate(BLOCKS):
        other = lax.rem(y + dy, chips_y) * 2 + lax.rem(core + dc, 2)
        mine, theirs = order[span], order[other]
        seen = jnp.where(theirs < mine, mask[mine, theirs], 0)
        hide[0, place] = jnp.where(seen > 0, 0.0, OUT_OF_MAX).astype(jnp.float32)
        hide[1, place] = jnp.where(seen > 0, 0.0, OUT_OF_SUM).astype(jnp.float32)

    span_rows = length // HALVES
    count = HALVES * len(BLOCKS)

    def rows_of(half):
        return pl.ds(pl.multiple_of(half * span_rows, span_rows), span_rows)

    def score(index, slot, columns):
        scores[slot, :, columns] = jnp.dot(
            blocks[lax.rem(index, len(BLOCKS)), 0, rows_of(index // len(BLOCKS))],
            queries_t[:, columns],
            preferred_element_type=jnp.float32,
        )

    def with_ones(values):
        return jnp.concatenate([values.T, jnp.ones((ONES, values.shape[0]), jnp.bfloat16)], axis=0)

    def weigh(block, columns, values, hide_max, hide_sum):
        before = top[:, columns]
        now = jnp.maximum(before, jnp.max(block, axis=0, keepdims=True) - hide_max)
        weights = jnp.exp2(block - (now + hide_sum)).astype(jnp.bfloat16)
        shrink = jnp.exp2(before - now)
        sums = jnp.dot(values, weights, preferred_element_type=jnp.float32)
        top[:, columns] = now
        mass[:, columns] = mass[:, columns] * shrink + sums[HD : HD + 1]
        total[:, columns] = total[:, columns] * shrink + sums[:HD]

    def weigh_at(index, slot, columns, values):
        place = lax.rem(index, len(BLOCKS))
        weigh(scores[slot, :, columns], columns, values, hide[0, place], hide[1, place])

    def values_at(index):
        return with_ones(blocks[lax.rem(index, len(BLOCKS)), 1, rows_of(index // len(BLOCKS))])

    top[...] = jnp.full_like(top, -3e38)
    mass[...] = jnp.zeros_like(mass)
    total[...] = jnp.zeros_like(total)
    sent = queries.at[pl.ds(0, length - tokens)]
    owns[3].wait()
    pltpu.make_async_copy(sent, sent, head_recv.at[0]).wait()
    queries_t[...] = queries[...].T
    await_core(0, 0)
    parts = [pl.ds(index * group, group) for index in range(ring_z)]
    for columns in parts:
        score(0, 0, columns)

    passing = {"staged": pass_staged, "near": pass_near, "far": pass_far, "core": await_core}

    def one_step(index, slot):
        for when, todo in WAITS:
            if when % 2 == slot:

                @pl.when(index == when)
                def _(todo=todo):
                    for what, *which in todo:
                        passing[what](*which)

        values = values_at(index)
        for columns in parts:
            score(index + 1, 1 - slot, columns)
            weigh_at(index, slot, columns, values)

    def two_steps(pair, carry):
        one_step(2 * pair, 0)
        one_step(2 * pair + 1, 1)
        return carry

    lax.fori_loop(0, count // 2 - 1, two_steps, 0)
    one_step(jnp.int32(count - 2), 0)
    owns[4].wait()
    pltpu.make_async_copy(sent, sent, head_recv.at[1]).wait()
    values = values_at(jnp.int32(count - 1))
    for columns in parts:
        own_scores[:, columns] = jnp.dot(
            blocks[OWN, 0], queries_t[:, columns], preferred_element_type=jnp.float32
        )
        weigh_at(jnp.int32(count - 1), 1, columns, values)

    owns[2].wait()
    pltpu.make_async_copy(sent, sent, head_recv.at[2]).wait()
    steps = lax.broadcasted_iota(jnp.int32, gates.shape, 0)
    gate = jnp.sum(jnp.where(steps == noise[span], gates[...], 0.0), axis=0, keepdims=True)
    values = with_ones(blocks[OWN, 1])
    for dz in (2, 1, 3, 0):
        rows = pl.ds(pl.multiple_of(lax.rem(z + dz, ring_z) * group, group), group)
        weigh(own_scores[:, rows], rows, values, 0.0, 0.0)
        attended = total[:, rows] / mass[:, rows]
        factor = lax.rsqrt(jnp.mean(attended * attended, axis=0, keepdims=True) + EPS)
        done[rows] = ((attended * factor).T * gate).astype(jnp.bfloat16)

        def send_out(dx, carry, dz=dz):
            other = peer(dz, dx)
            pltpu.make_async_remote_copy(
                src_ref=done.at[pl.ds(pl.multiple_of(other * tokens, tokens), tokens)],
                dst_ref=out.at[0, :, my_columns],
                send_sem=out_send,
                recv_sem=out_recv,
                device_id=(span, other, mp),
                device_id_type=MESH,
            ).start()
            return carry

        lax.fori_loop(1 if dz == 0 else 0, ring_x, send_out, 0)
    keep = pltpu.make_async_copy(done.at[my_rows], out.at[0, :, my_columns], local_sem.at[5])
    keep.start()
    keep.wait()

    for sem in (cache_send.at[0], cache_send.at[1], head_send.at[0], head_send.at[1], head_send.at[2]):
        pltpu.make_async_copy(sent, sent, sem).wait()
    whole = blocks.at[STAGED]
    for way in range(2):
        pltpu.make_async_copy(whole, whole, near_send.at[way]).wait()
        pltpu.make_async_copy(whole.at[0], whole.at[0], far_send.at[way]).wait()
    for index in range(chips_y):
        pltpu.make_async_copy(whole, whole, core_send.at[index]).wait()
    pltpu.make_async_copy(sent, sent, out_send).wait()
    pltpu.make_async_copy(sent, sent, out_recv).wait()


def shards(
    query,
    key,
    value,
    cache_key,
    cache_value,
    q_gain,
    k_gain,
    gate_table,
    span_order,
    noise_step,
    context_mask,
):
    spans, members = lax.axis_size("span"), lax.axis_size("seq")
    chips_y = spans // 2
    ring_x = 4
    ring_z = members // ring_x
    tokens, columns = query.shape[1:]
    length = tokens * members
    dma = pltpu.SemaphoreType.DMA
    in_hbm = pl.BlockSpec(memory_space=pltpu.HBM)
    in_vmem = pl.BlockSpec(memory_space=pltpu.VMEM)
    bf16, f32 = jnp.bfloat16, jnp.float32
    return pl.pallas_call(
        functools.partial(exchange_and_attend, chips_y, ring_z, ring_x),
        out_shape=jax.ShapeDtypeStruct(query.shape, bf16),
        in_specs=[in_hbm] * 11,
        out_specs=in_vmem,
        scratch_shapes=[
            pltpu.VMEM((2, columns), f32),
            pltpu.SMEM(span_order.shape, jnp.int32),
            pltpu.SMEM(noise_step.shape, jnp.int32),
            pltpu.SMEM(context_mask.shape, jnp.int32),
            pltpu.VMEM((5, tokens, columns), bf16),
            pltpu.VMEM((2, tokens, columns), bf16),
            pltpu.VMEM((2, tokens, HD), f32),
            pltpu.VMEM((gate_table.shape[0], HD), f32),
            pltpu.SMEM((2, len(BLOCKS)), f32),
            pltpu.VMEM((length, HD), bf16),
            pltpu.VMEM((HD, length), bf16),
            pltpu.VMEM((len(BLOCKS) + 2, 2, length, HD), bf16),
            pltpu.VMEM((2, length // HALVES, length), f32),
            pltpu.VMEM((length, length), f32),
            pltpu.VMEM((HD, length), f32),
            pltpu.VMEM((1, length), f32),
            pltpu.VMEM((1, length), f32),
            pltpu.VMEM((length, HD), bf16),
            dma((11,)),
            dma((6,)),
            dma,
            dma,
            dma((2,)),
            dma((ring_z,)),
            dma((3,)),
            dma((3,)),
            dma((2,)),
            dma((2, ring_z)),
            dma((2,)),
            dma((2, ring_z)),
            dma((chips_y,)),
            dma((chips_y, HALVES)),
            dma,
            dma,
        ],
        compiler_params=pltpu.CompilerParams(
            collective_id=0, has_side_effects=True, vmem_limit_bytes=63 << 20
        ),
        name="exchange_and_attend",
    )(
        query,
        key,
        value,
        cache_key,
        cache_value,
        q_gain,
        k_gain,
        gate_table,
        span_order,
        noise_step,
        context_mask,
    )


def solution(mesh):
    placed = (
        P("span", "seq", "mp"),
        P("span", "seq", "mp"),
        P("span", "seq", "mp"),
        P("span", "seq", "mp"),
        P("span", "seq", "mp"),
        P("mp"),
        P("mp"),
        P(None, "mp"),
        P(),
        P(),
        P(),
    )
    return jax.shard_map(
        shards, mesh=mesh, in_specs=placed, out_specs=P("span", "seq", "mp"), check_vma=False
    )
```

time: 85.4 us -> 60.5 us (0.71)
  Pallas kernels: 74.8 us -> 58.7 us
  local copies, waits for them, and re-layouts: 9.82 us -> 1.67 us
    pallas_call x1, Pallas kernels: 74.8 us -> 58.7 us  [shards(): pl.pallas_call(functools.partial(exchange_and_attend, chips_y, ring_z, ri...]
    unnamed x23 -> x1, local copies, waits for them, and re-layouts: 9.82 us -> 1.67 us
where the time goes in v1:
time: 60.5 us; the launch traced here: 60.4 us
  Pallas kernels  58.7 us (97%)
  local copies, waits for them, and re-layouts  1.67 us (3%)
    pallas_call x1, Pallas kernels, shards(): pl.pallas_call(functools.partial(exchange_and_attend, chips_y, ring_z, ri...  58.7 us
    unnamed x1, local copies, waits for them, and re-layouts  1.67 us

profile of v1, /device:TPU:2, one launch (start us, length us, event | category | flops | bytes accessed | tf_op | source)
XLA Modules:
  0.0 60.4 jit_solution(10835421523441032104)
XLA Ops:
  0.0 58.7 %exchange_and_attend.1 = bf16[1,64,2048]{2,1,0:T(8,128)(2,1)} custom-call(bf16[1,64,2048]{2,1,0:T(8,128)(2,1)} %query.1, bf16[1,64,2048]{2,1,0:T(8,128)(2,1)} %key.1, bf16[1,64,2048]{2,1,0:T(8,128)(2,1)} %value.1, bf16[1,64,2048]{2,1,0:T(8,128)(2,1)} %cache_key.1, bf16[1,64,2048]{2,1,0:T(8,128)(2,1)} %cache_value.1, f32[2048]{0:T(1024)} %q_gain.1, ...), custom_call_target="tpu_custom_call" | custom-call | tf_op jit(solution)/shard_map/exchange_and_attend/pallas_call | solution.py:468
  58.7 1.7 %copy.13 = bf16[1,64,2048]{2,1,0:T(8,128)(2,1)} copy(bf16[1,64,2048]{2,1,0:T(8,128)(2,1)} %exchange_and_attend.1) | data formatting | bytes 524288

commit v2 on v1

--- a/solution.py
+++ b/solution.py
@@ -14,7 +14,6 @@
 EPS = 1e-6
 Z_ORDER = (0, 1, 3, 2)
 HALVES = 2
-EARLY = 3
 BLOCKS = ((0, 1), (1, 0), (3, 0), (1, 1), (3, 1), (2, 0), (2, 1))
 OWN = len(BLOCKS)
 STAGED = OWN + 1
@@ -22,13 +21,12 @@
 FAR = 5
 ONES = 16
 WAITS = (
-    (1, (("core", 1, 0),)),
-    (2, (("core", 2, 0), ("staged", 3))),
-    (3, (("near", 2), ("far", 1))),
-    (4, (("core", 3, 0), ("far", 2))),
-    (5, (("near", 3),)),
+    (1, (("core", 1, 0), ("near", 3))),
+    (2, (("core", 2, 0),)),
+    (3, (("far", 2),)),
+    (4, (("core", 3, 0),)),
+    (5, (("far", 3),)),
     (6, (("core", 0, 1),)),
-    (8, (("far", 3),)),
     (9, (("core", 1, 1),)),
     (10, (("core", 2, 1),)),
     (12, (("core", 3, 1),)),
@@ -52,7 +50,7 @@
     span_order,
     noise_step,
     context_mask,
-    result,
+    out,
     gains,
     order,
     noise,
@@ -88,7 +86,6 @@
     out_send,
     out_recv,
 ):
-    out = result
     span = lax.axis_index("span")
     seq = lax.axis_index("seq")
     mp = lax.axis_index("mp")
@@ -202,7 +199,7 @@
 
         lax.fori_loop(1 if dz == 0 else 0, ring_x, send, 0)
 
-    for stage in range(EARLY):
+    for stage in range(ring_z):
         send_caches(stage)
 
     def to_core(source, target, stage, index):
@@ -304,9 +301,6 @@
         own.start()
         owns.append(own)
         send_heads(which, normed.at[which])
-        if which == 0:
-            for stage in range(EARLY, ring_z):
-                send_caches(stage)
     send_heads(2, raw.at[4])
 
     pass_staged(1)
@@ -314,6 +308,9 @@
     pass_staged(2)
     pass_near(1)
     pass_far(0)
+    pass_staged(3)
+    pass_near(2)
+    pass_far(1)
 
     for load in loads[4:8]:
         load.wait()
@@ -463,13 +460,12 @@
     length = tokens * members
     dma = pltpu.SemaphoreType.DMA
     in_hbm = pl.BlockSpec(memory_space=pltpu.HBM)
-    in_vmem = pl.BlockSpec(memory_space=pltpu.VMEM)
     bf16, f32 = jnp.bfloat16, jnp.float32
     return pl.pallas_call(
         functools.partial(exchange_and_attend, chips_y, ring_z, ring_x),
         out_shape=jax.ShapeDtypeStruct(query.shape, bf16),
         in_specs=[in_hbm] * 11,
-        out_specs=in_vmem,
+        out_specs=in_hbm,
         scratch_shapes=[
             pltpu.VMEM((2, columns), f32),
             pltpu.SMEM(span_order.shape, jnp.int32),

time: 60.5 us -> 58.5 us (0.967)
  Pallas kernels: 58.7 us -> 56.7 us
    pallas_call x1, Pallas kernels: 58.7 us -> 56.7 us  [shards(): pl.pallas_call(functools.partial(exchange_and_attend, chips_y, ring_z, ri...]
where the time goes in v2:
time: 58.5 us; the launch traced here: 58.4 us
  Pallas kernels  56.7 us (97%)
  local copies, waits for them, and re-layouts  1.67 us (3%)
    pallas_call x1, Pallas kernels, shards(): pl.pallas_call(functools.partial(exchange_and_attend, chips_y, ring_z, ri...  56.7 us
    unnamed x1, local copies, waits for them, and re-layouts  1.67 us

profile of v2, /device:TPU:2, one launch (start us, length us, event | category | flops | bytes accessed | tf_op | source)
XLA Modules:
  0.0 58.4 jit_solution(13542345669167521861)
XLA Ops:
  0.0 56.7 %exchange_and_attend.1 = bf16[1,64,2048]{2,1,0:T(8,128)(2,1)} custom-call(bf16[1,64,2048]{2,1,0:T(8,128)(2,1)} %query.1, bf16[1,64,2048]{2,1,0:T(8,128)(2,1)} %key.1, bf16[1,64,2048]{2,1,0:T(8,128)(2,1)} %value.1, bf16[1,64,2048]{2,1,0:T(8,128)(2,1)} %cache_key.1, bf16[1,64,2048]{2,1,0:T(8,128)(2,1)} %cache_value.1, f32[2048]{0:T(1024)} %q_gain.1, ...), custom_call_target="tpu_custom_call" | custom-call | tf_op jit(solution)/shard_map/exchange_and_attend/pallas_call | solution.py:464
  56.7 1.7 %copy.13 = bf16[1,64,2048]{2,1,0:T(8,128)(2,1)} copy(bf16[1,64,2048]{2,1,0:T(8,128)(2,1)} %exchange_and_attend.1) | data formatting | bytes 524288

commit v3 on v2

--- a/solution.py
+++ b/solution.py
@@ -139,9 +139,6 @@
                 (span_order, order),
                 (noise_step, noise),
                 (context_mask, mask),
-                (cache_key.at[0], raw.at[2]),
-                (cache_value.at[0], raw.at[3]),
-                (value.at[0], raw.at[4]),
             )
         )
     ]
@@ -156,16 +153,14 @@
         return jnp.sum(wide * wide, axis=-1, keepdims=True)
 
     squares[0] = jnp.where(lane < HD // 2, row_squares(0), row_squares(1))
-    for load in loads[8:]:
-        load.wait()
     owns = [
         pltpu.make_async_copy(
-            raw.at[2, :, my_columns], blocks.at[STAGED, 0, landing(0)], local_sem.at[0]
+            cache_key.at[0, :, my_columns], blocks.at[STAGED, 0, landing(0)], local_sem.at[0]
         ),
         pltpu.make_async_copy(
-            raw.at[3, :, my_columns], blocks.at[STAGED, 1, landing(0)], local_sem.at[1]
+            cache_value.at[0, :, my_columns], blocks.at[STAGED, 1, landing(0)], local_sem.at[1]
         ),
-        pltpu.make_async_copy(raw.at[4, :, my_columns], blocks.at[OWN, 1, landing(0)], local_sem.at[2]),
+        pltpu.make_async_copy(value.at[0, :, my_columns], blocks.at[OWN, 1, landing(0)], local_sem.at[2]),
     ]
     for own in owns:
         own.start()
@@ -188,7 +183,7 @@
             columns = pl.ds(pl.multiple_of(other * HD, HD), HD)
             for which in range(2):
                 pltpu.make_async_remote_copy(
-                    src_ref=raw.at[2 + which, :, columns],
+                    src_ref=(cache_key, cache_value)[which].at[0, :, columns],
                     dst_ref=blocks.at[STAGED, which, landing(stage)],
                     send_sem=cache_send.at[which],
                     recv_sem=cache_recv.at[stage],
@@ -301,7 +296,7 @@
         own.start()
         owns.append(own)
         send_heads(which, normed.at[which])
-    send_heads(2, raw.at[4])
+    send_heads(2, value.at[0])
 
     pass_staged(1)
     pass_near(0)
@@ -362,7 +357,7 @@
     pltpu.make_async_copy(sent, sent, head_recv.at[0]).wait()
     queries_t[...] = queries[...].T
     await_core(0, 0)
-    parts = [pl.ds(index * group, group) for index in range(ring_z)]
+    parts = [pl.ds(index * 2 * group, 2 * group) for index in range(ring_z // 2)]
     for columns in parts:
         score(0, 0, columns)
 
@@ -471,7 +466,7 @@
             pltpu.SMEM(span_order.shape, jnp.int32),
             pltpu.SMEM(noise_step.shape, jnp.int32),
             pltpu.SMEM(context_mask.shape, jnp.int32),
-            pltpu.VMEM((5, tokens, columns), bf16),
+            pltpu.VMEM((2, tokens, columns), bf16),
             pltpu.VMEM((2, tokens, columns), bf16),
             pltpu.VMEM((2, tokens, HD), f32),
             pltpu.VMEM((gate_table.shape[0], HD), f32),
@@ -485,7 +480,7 @@
             pltpu.VMEM((1, length), f32),
             pltpu.VMEM((1, length), f32),
             pltpu.VMEM((length, HD), bf16),
-            dma((11,)),
+            dma((8,)),
             dma((6,)),
             dma,
             dma,

time: 58.5 us -> 57.5 us (0.983)
  Pallas kernels: 56.7 us -> 55.7 us
    pallas_call x1, Pallas kernels: 56.7 us -> 55.7 us  [shards(): pl.pallas_call(functools.partial(exchange_and_attend, chips_y, ring_z, ri...]
where the time goes in v3:
time: 57.5 us; the launch traced here: 57.4 us
  Pallas kernels  55.7 us (97%)
  local copies, waits for them, and re-layouts  1.67 us (3%)
    pallas_call x1, Pallas kernels, shards(): pl.pallas_call(functools.partial(exchange_and_attend, chips_y, ring_z, ri...  55.7 us
    unnamed x1, local copies, waits for them, and re-layouts  1.67 us

profile of v3, /device:TPU:2, one launch (start us, length us, event | category | flops | bytes accessed | tf_op | source)
XLA Modules:
  0.0 57.4 jit_solution(15771447173530144440)
XLA Ops:
  0.0 55.7 %exchange_and_attend.1 = bf16[1,64,2048]{2,1,0:T(8,128)(2,1)} custom-call(bf16[1,64,2048]{2,1,0:T(8,128)(2,1)} %query.1, bf16[1,64,2048]{2,1,0:T(8,128)(2,1)} %key.1, bf16[1,64,2048]{2,1,0:T(8,128)(2,1)} %value.1, bf16[1,64,2048]{2,1,0:T(8,128)(2,1)} %cache_key.1, bf16[1,64,2048]{2,1,0:T(8,128)(2,1)} %cache_value.1, f32[2048]{0:T(1024)} %q_gain.1, ...), custom_call_target="tpu_custom_call" | custom-call | tf_op jit(solution)/shard_map/exchange_and_attend/pallas_call | solution.py:459
  55.7 1.7 %copy.13 = bf16[1,64,2048]{2,1,0:T(8,128)(2,1)} copy(bf16[1,64,2048]{2,1,0:T(8,128)(2,1)} %exchange_and_attend.1) | data formatting | bytes 524288

commit v4 on v3

--- a/solution.py
+++ b/solution.py
@@ -21,16 +21,15 @@
 FAR = 5
 ONES = 16
 WAITS = (
-    (1, (("core", 1, 0), ("near", 3))),
-    (2, (("core", 2, 0),)),
-    (3, (("far", 2),)),
-    (4, (("core", 3, 0),)),
-    (5, (("far", 3),)),
+    (1, (("core", 1, 0),)),
+    (2, (("core", 2, 0), ("far", 2))),
+    (4, (("core", 3, 0), ("far", 3))),
     (6, (("core", 0, 1),)),
     (9, (("core", 1, 1),)),
     (10, (("core", 2, 1),)),
     (12, (("core", 3, 1),)),
 )
+PIECES = 4
 OUT_OF_MAX = 1e30
 OUT_OF_SUM = 3e30
 
@@ -142,8 +141,14 @@
             )
         )
     ]
-    for load in loads:
+    for load in loads[2:]:
         load.start()
+    for which, source in enumerate((query, key)):
+        for piece in range(PIECES):
+            rows = pl.ds(piece * (tokens // PIECES), tokens // PIECES)
+            pltpu.make_async_copy(
+                source.at[0, rows], raw.at[which, rows], load_sem.at[which]
+            ).start()
     loads[0].wait()
     loads[1].wait()
     lane = lax.broadcasted_iota(jnp.int32, (tokens, HD), 1)
@@ -306,6 +311,7 @@
     pass_staged(3)
     pass_near(2)
     pass_far(1)
+    pass_near(3)
 
     for load in loads[4:8]:
         load.wait()

time: 57.5 us -> 57.4 us (level)
  no operation moved by 1% of the time
where the time goes in v4:
time: 57.4 us; the launch traced here: 57.2 us
  Pallas kernels  55.5 us (97%)
  local copies, waits for them, and re-layouts  1.67 us (3%)
    pallas_call x1, Pallas kernels, shards(): pl.pallas_call(functools.partial(exchange_and_attend, chips_y, ring_z, ri...  55.5 us
    unnamed x1, local copies, waits for them, and re-layouts  1.67 us

profile of v4, /device:TPU:2, one launch (start us, length us, event | category | flops | bytes accessed | tf_op | source)
XLA Modules:
  0.0 57.2 jit_solution(8309144365238166144)
XLA Ops:
  0.0 55.5 %exchange_and_attend.1 = bf16[1,64,2048]{2,1,0:T(8,128)(2,1)} custom-call(bf16[1,64,2048]{2,1,0:T(8,128)(2,1)} %query.1, bf16[1,64,2048]{2,1,0:T(8,128)(2,1)} %key.1, bf16[1,64,2048]{2,1,0:T(8,128)(2,1)} %value.1, bf16[1,64,2048]{2,1,0:T(8,128)(2,1)} %cache_key.1, bf16[1,64,2048]{2,1,0:T(8,128)(2,1)} %cache_value.1, f32[2048]{0:T(1024)} %q_gain.1, ...), custom_call_target="tpu_custom_call" | custom-call | tf_op jit(solution)/shard_map/exchange_and_attend/pallas_call | solution.py:465
  55.5 1.7 %copy.13 = bf16[1,64,2048]{2,1,0:T(8,128)(2,1)} copy(bf16[1,64,2048]{2,1,0:T(8,128)(2,1)} %exchange_and_attend.1) | data formatting | bytes 524288
